TPU v7x, 32 devices: a whole 2x2x4 slice. The times are simulated.
32 devices in a mesh: grp: 2 (over y), seq: 4 (over z), blk: 2 (over x), rep: 2 (over core).
Axes of the slice: x: 2, y: 2, z: 4, core: 2. Of those that a mesh axis runs over, the one named last changes fastest.
Arguments:
- q_proj: bfloat16 [8, 2048, 512], P(('grp', 'blk', 'rep'), 'seq'), parts along dimension 0, may hold values from -6 to 6
- k_proj: bfloat16 [8, 2048, 128], P(('grp', 'blk', 'rep'), 'seq'), parts along dimension 0, may hold values from -6 to 6
- v_proj: bfloat16 [8, 2048, 128], P(('grp', 'blk', 'rep'), 'seq'), parts along dimension 0, may hold values from -6 to 6
- q_gain: float32 [128], replicated, may hold values from 0.5 to 1.5
- k_gain: float32 [128], replicated, may hold values from 0.5 to 1.5
- out_weight: bfloat16 [512, 2560], P('seq'), may hold values from -0.25 to 0.25
- lengths: int32 [8, 1], P(('grp', 'blk', 'rep')), parts along dimension 0, may hold values from 512 to 2048, as said below
- query_emb: bfloat16 [512, 2560], P(('grp', 'blk')), parts along dimension 0, may hold values from -6 to 6
- teacher: float32 [512, 4], P(('grp', 'blk')), parts along dimension 0, may hold values from -16 to 16
Outputs:
- q_grad: bfloat16 [8, 2048, 512], P(('grp', 'blk', 'rep'), 'seq'), parts along dimension 0
- k_grad: bfloat16 [8, 2048, 128], P(('grp', 'blk', 'rep'), 'seq'), parts along dimension 0
- v_grad: bfloat16 [8, 2048, 128], P(('grp', 'blk', 'rep'), 'seq'), parts along dimension 0
- weight_grad: bfloat16 [1024, 2560], P(('grp', 'seq')), parts along dimension 0
- row_loss: float32 [512], P(('grp', 'blk')), parts along dimension 0
- col_loss: float32 [8], P('grp'), parts along dimension 0
There are 2 independent parts, one for each index of `grp`. A program takes and returns all parts, laid end to end along the dimension named above; an argument that names none is the same for every part. Nothing has to cross between parts.
Inputs may be any that keep to these rules, and one draw needn't show every extreme that they name: `lengths`: live tokens of each passage, counted from its first position; the rest is padding.
All inputs are finite; a program needn't handle non-finite values.
Results may differ from a plain program's by a relative error of at most 0.017.
Values may be sent and summed in bfloat16 or wider, within the bound.
A program may use at most 64 MiB of HBM per device.

v0:
```python
import math

import jax
import jax.numpy as jnp
from jax import lax
from jax.sharding import PartitionSpec as P

HD = 128
PASS_LEN = 2048


logit_divisor = 0.05


def rms_scale(wide):
    return lax.rsqrt(jnp.mean(wide * wide, axis=-1, keepdims=True) + 1e-06)


def normed(source, gain_weights):
    wide = source.astype(jnp.float32)
    return (wide * rms_scale(wide) * gain_weights).astype(jnp.bfloat16)


def norm_back(source, gain_weights, grad_out):
    wide = source.astype(jnp.float32)
    inv_rms = rms_scale(wide)
    scaled_grad = gain_weights * grad_out
    return (
        inv_rms * scaled_grad
        - wide * inv_rms**3 * jnp.mean(scaled_grad * wide, axis=-1, keepdims=True)
    ).astype(jnp.bfloat16)


def shards(q_proj, k_proj, v_proj, q_gain, k_gain, out_weight, lengths, query_emb, teacher):
    number_of_sequences = lax.axis_size("seq")
    blk_count = lax.axis_size("blk")
    tok_dev = q_proj.shape[1]
    heads_all = q_proj.shape[2] // HD
    kv_heads = k_proj.shape[2] // HD
    group_size = heads_all // kv_heads
    local_heads = out_weight.shape[0] // HD
    group_tok = tok_dev * number_of_sequences
    passes = group_tok // PASS_LEN
    pass_lens = lengths[0]
    inv_root = 1.0 / math.sqrt(HD)
    block_rows = min(512, PASS_LEN)
    block_count = PASS_LEN // block_rows

    def widen(rows):
        spread = jnp.broadcast_to(
            rows.reshape(tok_dev, kv_heads, 1, HD), (tok_dev, kv_heads, group_size, HD)
        )
        return spread.reshape(tok_dev, heads_all * HD)

    q_heads, k_heads, v_heads = (
        lax.all_to_all(q_proj[0], "seq", split_axis=1, concat_axis=0, tiled=True),
        lax.all_to_all(widen(k_proj[0]), "seq", split_axis=1, concat_axis=0, tiled=True),
        lax.all_to_all(widen(v_proj[0]), "seq", split_axis=1, concat_axis=0, tiled=True),
    )
    head_shape = (passes, PASS_LEN, local_heads, HD)
    q_raw = q_heads.reshape(head_shape)
    k_raw = k_heads.reshape(head_shape)
    v_all = v_heads.reshape(head_shape)
    q_unit = normed(q_raw, q_gain)
    k_unit = normed(k_raw, k_gain)
    positions = lax.iota(jnp.int32, PASS_LEN)
    passage = 0
    q_block = q_unit[passage]
    k_block = k_unit[passage]
    stored = []
    for attend_index in range(block_count):
        attend_ending = (attend_index + 1) * block_rows
        rows_here = q_block[attend_index * block_rows : attend_ending]
        logits = (
            jnp.einsum(
                "thd,uhd->htu",
                rows_here,
                k_block[:attend_ending],
                preferred_element_type=jnp.float32,
            )
            * inv_root
        )
        causal = (attend_index * block_rows + lax.iota(jnp.int32, block_rows))[:, None] >= lax.iota(
            jnp.int32, attend_ending
        )[None, :]
        powers = jnp.where(causal[None], jnp.exp(logits), 0.0)
        stored.append(
            lax.optimization_barrier(
                (powers / jnp.sum(powers, axis=2, keepdims=True)).astype(jnp.bfloat16)
            )
        )
    blocks = stored
    saved_blocks = [blocks]
    live_len = pass_lens[passage]
    live_mask = (positions < live_len).astype(jnp.bfloat16)
    col_weight = jnp.zeros((local_heads, PASS_LEN), jnp.float32)
    for index in range(block_count):
        ending = (index + 1) * block_rows
        column_part = jnp.einsum(
            "t,htu->hu",
            live_mask[index * block_rows : ending],
            blocks[index],
            preferred_element_type=jnp.float32,
        )
        col_weight = col_weight.at[:, :ending].add(column_part)
    col_weight = col_weight / live_len.astype(jnp.float32)
    pooled_list = [jnp.sum(col_weight.T[:, :, None] * v_all[passage].astype(jnp.float32), axis=0)]
    weight_list = [col_weight.astype(jnp.bfloat16)]
    pooled = jnp.stack(pooled_list)
    col_weights = jnp.stack(weight_list)
    pooled_flat = pooled.reshape(passes, local_heads * HD).astype(jnp.bfloat16)
    partial_value = jnp.dot(pooled_flat, out_weight, preferred_element_type=jnp.float32)
    summed = lax.psum(partial_value, "seq")
    inv_norm = lax.rsqrt(jnp.sum(summed * summed, axis=1, keepdims=True) + 1e-06)
    passage_unit = summed * inv_norm
    passage_all = lax.all_gather(
        passage_unit.astype(jnp.bfloat16), ("blk", "rep"), axis=0, tiled=True
    )
    query_wide = query_emb.astype(jnp.float32)
    request_unit_length = (
        query_wide * lax.rsqrt(jnp.sum(query_wide * query_wide, axis=1, keepdims=True) + 1e-06)
    ).astype(jnp.bfloat16)
    learner_similarities = (
        lax.dot_general(
            request_unit_length,
            passage_all,
            (((1,), (1,)), ((), ())),
            preferred_element_type=jnp.float32,
        )
        / logit_divisor
    )
    exp_student = jnp.exp(learner_similarities)
    exp_teacher = jnp.exp(teacher)
    row_student = jnp.sum(exp_student, axis=1, keepdims=True)
    row_teacher = jnp.sum(exp_teacher, axis=1, keepdims=True)
    gap = exp_teacher * (teacher - learner_similarities)
    col_student, col_teacher, col_gap = lax.psum(
        (jnp.sum(exp_student, axis=0), jnp.sum(exp_teacher, axis=0), jnp.sum(gap, axis=0)), "blk"
    )
    row_loss = (
        jnp.sum(gap, axis=1) / row_teacher[:, 0]
        - jnp.log(row_teacher[:, 0])
        + jnp.log(row_student[:, 0])
    )
    col_loss = col_gap / col_teacher - jnp.log(col_teacher) + jnp.log(col_student)
    query_total = query_emb.shape[0] * blk_count
    passage_total = teacher.shape[1]
    similarity_derivative = (
        (exp_student / row_student - exp_teacher / row_teacher) / query_total
        + (exp_student / col_student - exp_teacher / col_teacher) / passage_total
    ).astype(jnp.bfloat16)
    grad_block = lax.psum_scatter(
        (
            lax.dot_general(
                similarity_derivative,
                request_unit_length,
                (((0,), (0,)), ((), ())),
                preferred_element_type=jnp.float32,
            )
            / logit_divisor
        ).astype(jnp.bfloat16),
        "blk",
        scatter_dimension=0,
        tiled=True,
    ).astype(jnp.float32)
    representation_derivative = lax.dynamic_slice_in_dim(
        grad_block, lax.axis_index("rep") * passes, passes, 0
    )
    grad_sum = (
        (
            representation_derivative
            - passage_unit
            * jnp.sum(passage_unit * representation_derivative, axis=1, keepdims=True)
        )
        * inv_norm
    ).astype(jnp.bfloat16)
    pooled_every, grads_every = (
        lax.all_gather(pooled_flat, ("blk", "rep"), axis=0, tiled=True),
        lax.all_gather(grad_sum, ("blk", "rep"), axis=0, tiled=True),
    )
    weight_grad = lax.dot_general(
        pooled_every, grads_every, (((0,), (0,)), ((), ())), preferred_element_type=jnp.float32
    ).astype(jnp.bfloat16)
    grad_pool = lax.dot_general(
        grad_sum, out_weight, (((1,), (1,)), ((), ())), preferred_element_type=jnp.float32
    )
    pool_heads = grad_pool.reshape(passes, local_heads, HD)
    passage = 0
    blocks = saved_blocks[passage]
    q_block = q_unit[passage]
    k_block = k_unit[passage]
    live_len = pass_lens[passage]
    live_mask = (positions < live_len).astype(jnp.float32) / live_len.astype(jnp.float32)
    value_dot = jnp.sum(v_all[passage].astype(jnp.float32) * pool_heads[passage][None], axis=2).T
    grad_k_copy = jnp.zeros((PASS_LEN, local_heads, HD), jnp.float32)
    query_parts = []
    for index in range(block_count):
        ending = (index + 1) * block_rows
        stored_block = blocks[index]
        value_here = value_dot[:, None, :ending]
        mean_dot = jnp.sum(stored_block.astype(jnp.float32) * value_here, axis=2)
        local_live_mask = live_mask[index * block_rows : ending]
        grad_logits = (
            stored_block.astype(jnp.float32)
            * local_live_mask[None, :, None]
            * (value_here - mean_dot[:, :, None])
            * inv_root
        ).astype(jnp.bfloat16)
        query_parts.append(
            jnp.einsum(
                "htu,uhd->thd", grad_logits, k_block[:ending], preferred_element_type=jnp.float32
            )
        )
        key_part = jnp.einsum(
            "htu,thd->uhd",
            grad_logits,
            q_block[index * block_rows : ending],
            preferred_element_type=jnp.float32,
        )
        grad_k_copy = grad_k_copy.at[:ending].add(key_part)
    grad_q_unit = jnp.concatenate(query_parts, axis=0)
    q_list = [norm_back(q_raw[passage], q_gain, grad_q_unit)]
    k_list = [norm_back(k_raw[passage], k_gain, grad_k_copy)]
    q_terms = jnp.stack(q_list)
    k_terms = jnp.stack(k_list)
    flat_shape = (group_tok, local_heads * HD)

    def narrow(terms):
        wide = terms.astype(jnp.float32).reshape(tok_dev, kv_heads, group_size, HD)
        return jnp.sum(wide, axis=2).astype(jnp.bfloat16).reshape(tok_dev, kv_heads * HD)

    q_back, k_back, v_back = (
        lax.all_to_all(q_terms.reshape(flat_shape), "seq", split_axis=0, concat_axis=1, tiled=True),
        lax.all_to_all(k_terms.reshape(flat_shape), "seq", split_axis=0, concat_axis=1, tiled=True),
        lax.all_to_all(
            (col_weights.astype(jnp.float32).transpose(0, 2, 1)[..., None] * pool_heads[:, None])
            .astype(jnp.bfloat16)
            .reshape(flat_shape),
            "seq",
            split_axis=0,
            concat_axis=1,
            tiled=True,
        ),
    )
    k_out = narrow(k_back)
    v_out = narrow(v_back)
    return (q_back[None], k_out[None], v_out[None], weight_grad, row_loss, col_loss)


def solution(mesh):
    placed = (
        P(("grp", "blk", "rep"), "seq", None),
        P(("grp", "blk", "rep"), "seq", None),
        P(("grp", "blk", "rep"), "seq", None),
        P(),
        P(),
        P("seq", None),
        P(("grp", "blk", "rep"), None),
        P(("grp", "blk"), None),
        P(("grp", "blk"), None),
    )
    return jax.shard_map(
        shards,
        mesh=mesh,
        in_specs=placed,
        out_specs=(
            P(("grp", "blk", "rep"), "seq", None),
            P(("grp", "blk", "rep"), "seq", None),
            P(("grp", "blk", "rep"), "seq", None),
            P(("grp", "seq"), None),
            P(("grp", "blk")),
            P("grp"),
        ),
        check_vma=False,
    )
```

profile of v0, /device:TPU:0, one launch (start us, length us, event | category | flops | bytes accessed | tf_op | source)
XLA Modules:
  0.0 180.6 jit_solution(1321558911935933446)
XLA Ops:
  0.7 1.1 copy.44
  1.8 0.8 broadcast_in_dim.25
  2.7 6.3 %all-to-all-start.1 = ((bf16[512,4,128]{0,2,1:T(8,128)(2,1)}), bf16[512,4,128]{0,2,1:T(8,128)(2,1)S(1)}, u32[]{:S(2)}, u32[]{:S(2)}) async-start(bf16[512,4,128]{0,2,1:T(8,128)(2,1)} %broadcast_in_dim.25), calls=%async_computation.1 | async-start | bytes 1048576 | tf_op jit(solution)/shard_map/all_to_all | solution.py:57
  9.0 1.0 copy.42
  10.7 12.7 %all-to-all-done.1 = bf16[512,4,128]{0,2,1:T(8,128)(2,1)S(1)} async-done(((bf16[512,4,128]{0,2,1:T(8,128)(2,1)}), bf16[512,4,128]{0,2,1:T(8,128)(2,1)S(1)}, u32[]{:S(2)}, u32[]{:S(2)}) %all-to-all-start.1) | async-done | bytes 524320 | tf_op jit(solution)/shard_map/all_to_all | solution.py:57
  23.5 3.5 %all-to-all-start = ((bf16[512,4,128]{0,2,1:T(8,128)(2,1)}), bf16[512,4,128]{0,2,1:T(8,128)(2,1)S(1)}, u32[]{:S(2)}, u32[]{:S(2)}) async-start(bf16[512,4,128]{0,2,1:T(8,128)(2,1)} %bitcast), calls=%async_computation | async-start | bytes 1048576 | tf_op jit(solution)/shard_map/all_to_all | solution.py:56
  28.3 0.6 compare_reduce_fusion.2
  28.9 0.6 compare_reduce_fusion
  29.8 0.6 fusion.94
  31.1 9.8 %all-to-all-done = bf16[512,4,128]{0,2,1:T(8,128)(2,1)S(1)} async-done(((bf16[512,4,128]{0,2,1:T(8,128)(2,1)}), bf16[512,4,128]{0,2,1:T(8,128)(2,1)S(1)}, u32[]{:S(2)}, u32[]{:S(2)}) %all-to-all-start) | async-done | bytes 524320 | tf_op jit(solution)/shard_map/all_to_all | solution.py:56
  40.9 0.9 broadcast_in_dim.29
  41.8 4.3 %all-to-all-start.2 = ((bf16[512,4,128]{2,0,1:T(8,128)(2,1)}), bf16[512,4,128]{2,0,1:T(8,128)(2,1)}, u32[]{:S(2)}, u32[]{:S(2)}) async-start(bf16[512,4,128]{2,0,1:T(8,128)(2,1)} %broadcast_in_dim.29), calls=%async_computation.2 | async-start | bytes 1048576 | tf_op jit(solution)/shard_map/all_to_all | solution.py:58
  46.8 0.6 add_rsqrt_fusion
  47.9 1.4 fusion.96
  49.9 0.6 copy-done.4
  51.4 0.7 fusion.98
  52.5 1.0 fusion.99
  54.1 0.7 broadcast_select_fusion.1
  54.9 0.9 fusion.35
  55.8 1.0 fusion.16
  56.8 1.0 convert_reduce_fusion
  57.8 2.3 %all-to-all-done.2 = bf16[512,4,128]{2,0,1:T(8,128)(2,1)} async-done(((bf16[512,4,128]{2,0,1:T(8,128)(2,1)}), bf16[512,4,128]{2,0,1:T(8,128)(2,1)}, u32[]{:S(2)}, u32[]{:S(2)}) %all-to-all-start.2) | async-done | bytes 524320 | tf_op jit(solution)/shard_map/all_to_all | solution.py:58
  60.1 1.1 convert_element_type.407
  61.2 1.0 copy-done.11
  63.3 16.8 %psum.28 = f32[1,2560]{1,0:T(1,128)S(1)} all-reduce(f32[1,2560]{1,0:T(1,128)S(1)} %fusion.77), channel_id=1, replica_groups=mesh['grp'=2,'seq'=4,'blk'=2,'rep'=2] {'seq'}, use_global_device_ids=true, to_apply=%region_11.12 | all-reduce | flops 2560 | bytes 20480 | tf_op jit(solution)/shard_map/psum | solution.py:113
  80.1 0.6 multiply_reduce_fusion.3
  81.4 5.2 %all-gather.1 = bf16[4,1,2560]{2,1,0:T(2,128)(2,1)S(1)} all-gather(bf16[1,1,2560]{2,1,0:T(2,128)(2,1)S(1)} %convert_bitcast_fusion.1), channel_id=1, replica_groups=mesh['grp'=2,'seq'=4,'blk'=2,'rep'=2] {'blk','rep'}, dimensions={0}, use_global_device_ids=true | all-gather | bytes 25600 | tf_op jit(solution)/shard_map/all_gather | solution.py:116
  86.6 2.0 %fusion.80 = (f32[4]{0:T(128)S(1)}, f32[128]{0:T(128)}, f32[4]{0:T(128)S(1)}, f32[128]{0:T(128)S(1)}, f32[4]{0:T(128)S(1)}, /*index=5*/f32[128]{0:T(128)S(1)}, f32[128,4]{0,1:T(4,128)S(1)}) fusion(f32[128,4]{0,1:T(4,128)S(1)} %copy-done.55, bf16[4,1,2560]{2,1,0:T(2,128)(2,1)S(1)} %all-gather.1, bf16[128,2560]{1,0:T(8,128)(2,1)} %param.36, ...), kind=kOutput, calls=%fused_computation.165 | convolution fusion | flops 3608692 | bytes 682032 | tf_op jit(solution)/shard_map/dot_general | solution.py:124
  88.6 5.4 %all-reduce.3 = (f32[4]{0:T(128)S(1)}, f32[4]{0:T(128)S(1)}, f32[4]{0:T(128)}) all-reduce(f32[4]{0:T(128)S(1)} %get-tuple-element.140, f32[4]{0:T(128)S(1)} %get-tuple-element.138, f32[4]{0:T(128)S(1)} %get-tuple-element.136), channel_id=1, replica_groups=mesh['grp'=2,'seq'=4,'blk'=2,'rep'=2] {'blk'}, use_global_device_ids=true, to_apply=%region_18.19 | all-reduce | flops 12 | bytes 96 | tf_op jit(solution)/shard_map/psum | solution.py:137
  94.1 1.4 fusion.4
  95.5 8.3 %all-reduce.2 = bf16[4,2560]{1,0:T(4,128)(2,1)S(1)} all-reduce(bf16[4,2560]{1,0:T(4,128)(2,1)S(1)} %fusion.4), channel_id=3, replica_groups=mesh['grp'=2,'seq'=4,'blk'=2,'rep'=2] {'blk'}, use_global_device_ids=true, to_apply=%region_19.20.clone | all-reduce | flops 10240 | bytes 40960
  103.7 0.6 multiply_reduce_fusion.2
  104.4 0.7 subtract_multiply_fusion
  105.9 1.6 fusion.44
  108.6 2.1 %convolution_bitcast_fusion.3 = f32[512,1,128]{0,2,1:T(8,128)} fusion(bf16[1,2048,1,128]{3,1,2,0:T(8,128)(2,1)} %copy-done.19, bf16[1,512,512]{1,2,0:T(8,128)(2,1)S(1)} %fusion.55, f32[512]{0:T(512)S(1)} %fusion.39, f32[512]{0:T(512)S(1)} %bitcast.270, f32[512]{0:T(512)S(1)} %get-tuple-element.148), kind=kOutput, calls=%fused_computation.61 | convolution fusion | flops 68681728 | bytes 923648 | tf_op jit(solution)/shard_map/htu,thd->uhd/dot_general | solution.py:214
  110.8 0.8 fusion.22
  112.0 1.3 fusion.87
  113.3 0.9 copy-done.8
  114.9 0.9 fusion.56
  115.9 0.7 fusion.59
  116.6 0.7 copy-done.18
  117.3 1.1 pad_maximum_fusion
  118.4 2.5 %copy.54 = f32[2048,128]{1,0:T(8,128)} copy(f32[2048,128]{0,1:T(8,128)} %pad_maximum_fusion) | data formatting | bytes 2097152 | tf_op jit(solution)/shard_map/concatenate | solution.py:221
  120.9 1.3 copy.55
  122.3 1.6 fusion.42
  123.9 2.9 %fusion.49 = bf16[4,512,128]{2,1,0:T(8,128)(2,1)} fusion(f32[4,512,128]{2,1,0:T(8,128)} %bitcast.241, bf16[512,4,128]{2,0,1:T(8,128)(2,1)} %copy-done.15, f32[4,512]{1,0:T(4,128)S(1)} %div.160, f32[4,512]{1,0:T(4,128)} %get-tuple-element.147, f32[128]{0:T(128)} %param.32, f32[4,512]{1,0:T(4,128)} %get-tuple-element.145), kind=kLoop, calls=%fused_computation.86 | loop fusion | flops 1835008 | bytes 2122240 | tf_op jit(solution)/shard_map/convert_element_type | solution.py:31
  126.8 2.1 %copy.48 = bf16[4,512,128]{1,2,0:T(8,128)(2,1)} copy(bf16[4,512,128]{2,1,0:T(8,128)(2,1)} %fusion.49) | data formatting | bytes 1048576 | tf_op jit(solution)/shard_map/convert_element_type | solution.py:31
  128.9 4.1 %all-to-all-start.3 = ((bf16[4,512,128]{1,2,0:T(8,128)(2,1)}), bf16[4,512,128]{1,2,0:T(8,128)(2,1)}, u32[]{:S(2)}, u32[]{:S(2)}) async-start(bf16[4,512,128]{1,2,0:T(8,128)(2,1)} %copy.48), calls=%async_computation.3 | async-start | bytes 1048576 | tf_op jit(solution)/shard_map/all_to_all | solution.py:233
  133.1 1.3 copy.56
  134.5 2.0 %fusion.33 = f32[2048,1,128]{0,2,1:T(8,128)S(1)} fusion(f32[2048,1,128]{0,2,1:T(8,128)S(1)} %scatter-add.25, bf16[1,2048,1,128]{3,1,2,0:T(8,128)(2,1)} %copy-done.19, bf16[1,512,1024]{2,1,0:T(8,128)(2,1)} %copy-done.12, f32[512]{0:T(512)} %copy-done.41, f32[1024]{0:T(1024)} %bitcast.267, f32[512]{0:T(512)} %get-tuple-element.151), kind=kOutput, calls=%fused_computation.60 | convolution fusion | flops 137494528 | bytes 2236416 | tf_op jit(solution)/shard_map/htu,thd->uhd/dot_general | solution.py:214
  136.5 0.9 fusion.12
  137.5 0.6 copy-done.2
  139.6 0.9 copy.50
  140.5 4.7 %all-to-all-done.3 = bf16[4,512,128]{1,2,0:T(8,128)(2,1)} async-done(((bf16[4,512,128]{1,2,0:T(8,128)(2,1)}), bf16[4,512,128]{1,2,0:T(8,128)(2,1)}, u32[]{:S(2)}, u32[]{:S(2)}) %all-to-all-start.3) | async-done | bytes 524320 | tf_op jit(solution)/shard_map/all_to_all | solution.py:233
  145.2 3.5 %all-to-all-start.4 = ((bf16[4,512,128]{1,2,0:T(8,128)(2,1)}), bf16[4,512,128]{1,2,0:T(8,128)(2,1)S(1)}, u32[]{:S(2)}, u32[]{:S(2)}) async-start(bf16[4,512,128]{1,2,0:T(8,128)(2,1)} %copy.50), calls=%async_computation.4 | async-start | bytes 1048576 | tf_op jit(solution)/shard_map/all_to_all | solution.py:234
  148.7 1.1 multiply_convert_fusion
  149.8 11.1 %all-to-all-done.4 = bf16[4,512,128]{1,2,0:T(8,128)(2,1)S(1)} async-done(((bf16[4,512,128]{1,2,0:T(8,128)(2,1)}), bf16[4,512,128]{1,2,0:T(8,128)(2,1)S(1)}, u32[]{:S(2)}, u32[]{:S(2)}) %all-to-all-start.4) | async-done | bytes 524320 | tf_op jit(solution)/shard_map/all_to_all | solution.py:234
  160.9 3.5 %all-to-all-start.5 = ((bf16[4,512,128]{2,1,0:T(8,128)(2,1)}), bf16[4,512,128]{2,1,0:T(8,128)(2,1)S(1)}, u32[]{:S(2)}, u32[]{:S(2)}) async-start(bf16[4,512,128]{2,1,0:T(8,128)(2,1)} %multiply_convert_fusion), calls=%async_computation.5 | async-start | bytes 1048576 | tf_op jit(solution)/shard_map/all_to_all | solution.py:235
  164.4 5.0 %all-gather.2 = bf16[4,1,128]{2,1,0:T(2,128)(2,1)S(1)} all-gather(bf16[1,1,128]{2,1,0:T(2,128)(2,1)S(1)} %bitcast.273), channel_id=2, replica_groups=mesh['grp'=2,'seq'=4,'blk'=2,'rep'=2] {'blk','rep'}, dimensions={0}, use_global_device_ids=true | all-gather | bytes 1280 | tf_op jit(solution)/shard_map/all_gather | solution.py:178
  169.4 5.2 %all-gather.3 = bf16[4,1,2560]{2,1,0:T(2,128)(2,1)S(1)} all-gather(bf16[1,1,2560]{2,1,0:T(2,128)(2,1)S(1)} %bitcast.262), channel_id=1, replica_groups=mesh['grp'=2,'seq'=4,'blk'=2,'rep'=2] {'blk','rep'}, dimensions={0}, use_global_device_ids=true | all-gather | bytes 25600 | tf_op jit(solution)/shard_map/all_gather | solution.py:179
  175.7 1.2 convolution_convert_fusion
  176.9 2.0 %copy.52 = bf16[1,512,512]{2,1,0:T(8,128)(2,1)} copy(bf16[1,512,512]{1,2,0:T(8,128)(2,1)} %bitcast.63) | data formatting | bytes 1048576
  179.1 0.8 copy.53
  179.8 0.7 reduce_sum.261
  (165 shorter events, 12.0 us)
Async XLA Ops:
  0.6 62.5 %copy-start = (bf16[128,2560]{1,0:T(8,128)(2,1)S(1)}, bf16[128,2560]{1,0:T(8,128)(2,1)}, u32[]{:S(2)}) copy-start(bf16[128,2560]{1,0:T(8,128)(2,1)} %param.34) | copy-start | bytes 1966084
  0.6 26.4 %copy-start.56 = (u32[32]{0:T(128)S(1)}, u32[32]{0:T(128)}, u32[]{:S(2)}) copy-start(u32[32]{0:T(128)} %constant.272) | copy-start | bytes 388
  0.7 8.3 %copy-start.22 = (bf16[1,512,512]{2,1,0:T(8,128)(2,1)S(1)}, bf16[1,512,512]{2,1,0:T(8,128)(2,1)}, u32[]{:S(2)}) copy-start(bf16[1,512,512]{2,1,0:T(8,128)(2,1)} %param.29) | copy-start | bytes 1572868
  0.7 28.9 %copy-start.21 = (bf16[128,2560]{1,0:T(8,128)(2,1)S(1)}, bf16[128,2560]{1,0:T(8,128)(2,1)}, u32[]{:S(2)}) copy-start(bf16[128,2560]{1,0:T(8,128)(2,1)} %param.36) | copy-start | bytes 1966084
  2.7 20.8 %all-to-all-start.1 = ((bf16[512,4,128]{0,2,1:T(8,128)(2,1)}), bf16[512,4,128]{0,2,1:T(8,128)(2,1)S(1)}, u32[]{:S(2)}, u32[]{:S(2)}) async-start(bf16[512,4,128]{0,2,1:T(8,128)(2,1)} %broadcast_in_dim.25), calls=%async_computation.1 | async-start | bytes 1048576 | tf_op jit(solution)/shard_map/all_to_all | solution.py:57
  23.5 17.4 %all-to-all-start = ((bf16[512,4,128]{0,2,1:T(8,128)(2,1)}), bf16[512,4,128]{0,2,1:T(8,128)(2,1)S(1)}, u32[]{:S(2)}, u32[]{:S(2)}) async-start(bf16[512,4,128]{0,2,1:T(8,128)(2,1)} %bitcast), calls=%async_computation | async-start | bytes 1048576 | tf_op jit(solution)/shard_map/all_to_all | solution.py:56
  26.9 14.0 %copy-start.26 = (bf16[1,512,128]{2,1,0:T(8,128)(2,1)S(1)}, bf16[1,512,128]{2,1,0:T(8,128)(2,1)}, u32[]{:S(2)}) copy-start(bf16[1,512,128]{2,1,0:T(8,128)(2,1)} %param.31) | copy-start | bytes 393220
  30.7 17.1 %copy-start.3 = (f32[512,4,128]{2,0,1:T(8,128)}, f32[512,4,128]{2,0,1:T(8,128)S(1)}, u32[]{:S(2)}) copy-start(f32[512,4,128]{2,0,1:T(8,128)S(1)} %convert_element_type.405) | copy-start | bytes 3145732
  41.8 5.8 %copy-start.31 = (f32[128]{0:T(128)S(1)}, f32[128]{0:T(128)}, u32[]{:S(2)}) copy-start(f32[128]{0:T(128)} %param.32) | copy-start | bytes 1540
  41.8 18.3 %all-to-all-start.2 = ((bf16[512,4,128]{2,0,1:T(8,128)(2,1)}), bf16[512,4,128]{2,0,1:T(8,128)(2,1)}, u32[]{:S(2)}, u32[]{:S(2)}) async-start(bf16[512,4,128]{2,0,1:T(8,128)(2,1)} %broadcast_in_dim.29), calls=%async_computation.2 | async-start | bytes 1048576 | tf_op jit(solution)/shard_map/all_to_all | solution.py:58
  46.3 3.0 %copy-start.15 = (bf16[512,4,128]{2,0,1:T(8,128)(2,1)}, bf16[512,4,128]{2,0,1:T(8,128)(2,1)S(1)}, u32[]{:S(2)}) copy-start(bf16[512,4,128]{2,0,1:T(8,128)(2,1)S(1)} %copy.43) | copy-start | bytes 1572868
  46.3 1.6 copy-start.32
  46.4 1.1 copy-start.9
  47.9 4.5 %copy-start.19 = (bf16[1,2048,1,128]{3,1,2,0:T(8,128)(2,1)}, bf16[1,2048,1,128]{3,1,2,0:T(8,128)(2,1)S(1)}, u32[]{:S(2)}) copy-start(bf16[1,2048,1,128]{3,1,2,0:T(8,128)(2,1)S(1)} %multiply_convert_fusion.2) | copy-start | bytes 1572868
  49.3 1.2 copy-start.4
  50.9 1.5 copy-start.23
  52.4 2.4 %copy-start.12 = (bf16[1,512,1024]{2,1,0:T(8,128)(2,1)}, bf16[1,512,1024]{2,1,0:T(8,128)(2,1)S(1)}, u32[]{:S(2)}) copy-start(bf16[1,512,1024]{2,1,0:T(8,128)(2,1)S(1)} %fusion.50) | copy-start | bytes 3145732
  53.9 1.9 %copy-start.7 = (bf16[1,512,1536]{2,1,0:T(8,128)(2,1)}, bf16[1,512,1536]{2,1,0:T(8,128)(2,1)S(1)}, u32[]{:S(2)}) copy-start(bf16[1,512,1536]{2,1,0:T(8,128)(2,1)S(1)} %fusion.27) | copy-start | bytes 4718596
  57.8 28.9 %copy-start.55 = (f32[128,4]{0,1:T(4,128)S(1)}, f32[128,4]{0,1:T(4,128)}, u32[]{:S(2)}) copy-start(f32[128,4]{0,1:T(4,128)} %param.37) | copy-start | bytes 6148
  61.2 1.0 copy-start.11
  62.5 0.5 copy-start.37
  88.6 19.3 %copy-start.46 = (f32[128]{0:T(128)}, f32[128]{0:T(128)S(1)}, u32[]{:S(2)}) copy-start(f32[128]{0:T(128)S(1)} %get-tuple-element.139) | copy-start | bytes 1540
  88.6 19.3 %copy-start.48 = (f32[128]{0:T(128)}, f32[128]{0:T(128)S(1)}, u32[]{:S(2)}) copy-start(f32[128]{0:T(128)S(1)} %get-tuple-element.141) | copy-start | bytes 1540
  94.1 9.7 %copy-start.50 = (f32[4]{0:T(128)}, f32[4]{0:T(128)S(1)}, u32[]{:S(2)}) copy-start(f32[4]{0:T(128)S(1)} %get-tuple-element.142) | copy-start | bytes 52
  94.1 9.7 %copy-start.52 = (f32[4]{0:T(128)}, f32[4]{0:T(128)S(1)}, u32[]{:S(2)}) copy-start(f32[4]{0:T(128)S(1)} %get-tuple-element.143) | copy-start | bytes 52
  105.0 3.1 %copy-start.27 = (bf16[1,2560]{1,0:T(2,128)(2,1)}, bf16[1,2560]{1,0:T(2,128)(2,1)S(1)}, u32[]{:S(2)}) copy-start(bf16[1,2560]{1,0:T(2,128)(2,1)S(1)} %subtract_multiply_fusion) | copy-start | bytes 15364
  105.1 3.1 %copy-start.24 = (bf16[1,2048,1,128]{3,1,2,0:T(8,128)(2,1)S(1)}, bf16[1,2048,1,128]{3,1,2,0:T(8,128)(2,1)}, u32[]{:S(2)}) copy-start(bf16[1,2048,1,128]{3,1,2,0:T(8,128)(2,1)} %copy-done.23) | copy-start | bytes 1572868
  105.3 0.5 copy-start.35
  108.0 7.9 %copy-start.30 = (f32[1,1024]{1,0:T(1,128)}, f32[1,1024]{1,0:T(1,128)S(1)}, u32[]{:S(2)}) copy-start(f32[1,1024]{1,0:T(1,128)S(1)} %slice.261) | copy-start | bytes 12292
  108.6 7.9 %copy-start.16 = (f32[128,512]{1,0:T(8,128)}, f32[128,512]{1,0:T(8,128)S(1)}, u32[]{:S(2)}) copy-start(f32[128,512]{1,0:T(8,128)S(1)} %fusion.60) | copy-start | bytes 786436
  110.8 1.2 copy-start.5
  110.8 1.2 copy-start.33
  112.0 2.6 %copy-start.1 = (bf16[512,2048]{1,0:T(8,128)(2,1)}, bf16[512,2048]{1,0:T(8,128)(2,1)S(1)}, u32[]{:S(2)}) copy-start(bf16[512,2048]{1,0:T(8,128)(2,1)S(1)} %fusion.22) | copy-start | bytes 6291460
  112.0 2.2 %copy-start.8 = (bf16[1,512,1536]{2,1,0:T(8,128)(2,1)S(1)}, bf16[1,512,1536]{2,1,0:T(8,128)(2,1)}, u32[]{:S(2)}) copy-start(bf16[1,512,1536]{2,1,0:T(8,128)(2,1)} %copy-done.7) | copy-start | bytes 4718596
  112.0 2.6 %copy-start.13 = (bf16[1,512,1024]{2,1,0:T(8,128)(2,1)S(1)}, bf16[1,512,1024]{2,1,0:T(8,128)(2,1)}, u32[]{:S(2)}) copy-start(bf16[1,512,1024]{2,1,0:T(8,128)(2,1)} %copy-done.12) | copy-start | bytes 3145732
  114.2 0.8 copy-start.42
  114.5 1.3 copy-start.39
  114.8 1.0 copy-start.41
  114.9 0.9 copy-start.44
  115.8 0.7 copy-start.17
  116.5 0.7 copy-start.18
  117.3 3.7 %copy-start.10 = (f32[512,4,128]{2,0,1:T(8,128)S(1)}, f32[512,4,128]{2,0,1:T(8,128)}, u32[]{:S(2)}) copy-start(f32[512,4,128]{2,0,1:T(8,128)} %copy-done.9) | copy-start | bytes 3145732
  123.9 9.2 %copy-start.6 = (f32[512,4,128]{2,0,1:T(8,128)S(1)}, f32[512,4,128]{2,0,1:T(8,128)}, u32[]{:S(2)}) copy-start(f32[512,4,128]{2,0,1:T(8,128)} %copy-done.3) | copy-start | bytes 3145732
  126.8 7.6 %copy-start.25 = (f32[512,1,128]{0,2,1:T(8,128)S(1)}, f32[512,1,128]{0,2,1:T(8,128)}, u32[]{:S(2)}) copy-start(f32[512,1,128]{0,2,1:T(8,128)} %convolution_bitcast_fusion.3) | copy-start | bytes 786436
  128.9 16.3 %all-to-all-start.3 = ((bf16[4,512,128]{1,2,0:T(8,128)(2,1)}), bf16[4,512,128]{1,2,0:T(8,128)(2,1)}, u32[]{:S(2)}, u32[]{:S(2)}) async-start(bf16[4,512,128]{1,2,0:T(8,128)(2,1)} %copy.48), calls=%async_computation.3 | async-start | bytes 1048576 | tf_op jit(solution)/shard_map/all_to_all | solution.py:233
  134.4 2.1 %copy-start.20 = (bf16[1,2048,1,128]{3,1,2,0:T(8,128)(2,1)S(1)}, bf16[1,2048,1,128]{3,1,2,0:T(8,128)(2,1)}, u32[]{:S(2)}) copy-start(bf16[1,2048,1,128]{3,1,2,0:T(8,128)(2,1)} %copy-done.19) | copy-start | bytes 1572868
  134.4 2.1 %copy-start.40 = (f32[512]{0:T(512)S(1)}, f32[512]{0:T(512)}, u32[]{:S(2)}) copy-start(f32[512]{0:T(512)} %copy-done.39) | copy-start | bytes 6148
  134.4 2.1 %copy-start.43 = (f32[512]{0:T(512)S(1)}, f32[512]{0:T(512)}, u32[]{:S(2)}) copy-start(f32[512]{0:T(512)} %get-tuple-element.150) | copy-start | bytes 6148
  136.5 1.6 copy-start.2
  136.5 1.8 %copy-start.14 = (f32[2048,1,128]{0,2,1:T(8,128)S(1)}, f32[2048,1,128]{0,2,1:T(8,128)}, u32[]{:S(2)}) copy-start(f32[2048,1,128]{0,2,1:T(8,128)} %copy.56) | copy-start | bytes 3145732
  136.5 1.8 %copy-start.34 = (f32[128]{0:T(128)S(1)}, f32[128]{0:T(128)}, u32[]{:S(2)}) copy-start(f32[128]{0:T(128)} %param.33) | copy-start | bytes 1540
  139.1 9.6 %copy-start.29 = (f32[2048]{0:T(1024)S(1)}, f32[2048]{0:T(1024)}, u32[]{:S(2)}) copy-start(f32[2048]{0:T(1024)} %get-tuple-element.167) | copy-start | bytes 24580
  139.1 9.6 %copy-start.36 = (f32[128]{0:T(128)S(1)}, f32[128]{0:T(128)}, u32[]{:S(2)}) copy-start(f32[128]{0:T(128)} %copy-done.35) | copy-start | bytes 1540
  139.5 24.9 %copy-start.38 = (bf16[128]{0:T(256)(128)(2,1)S(1)}, bf16[128]{0:T(256)(128)(2,1)}, u32[]{:S(2)}) copy-start(bf16[128]{0:T(256)(128)(2,1)} %copy-done.37) | copy-start | bytes 772
  139.5 29.9 %copy-start.28 = (bf16[1,2560]{1,0:T(2,128)(2,1)S(1)}, bf16[1,2560]{1,0:T(2,128)(2,1)}, u32[]{:S(2)}) copy-start(bf16[1,2560]{1,0:T(2,128)(2,1)} %copy-done.27) | copy-start | bytes 15364
  139.5 35.1 %copy-start.45 = (f32[128]{0:T(128)S(1)}, f32[128]{0:T(128)}, u32[]{:S(2)}) copy-start(f32[128]{0:T(128)} %get-tuple-element.137) | copy-start | bytes 1540
  139.6 35.1 %copy-start.47 = (f32[128]{0:T(128)S(1)}, f32[128]{0:T(128)}, u32[]{:S(2)}) copy-start(f32[128]{0:T(128)} %copy-done.46) | copy-start | bytes 1540
  139.6 35.1 %copy-start.49 = (f32[128]{0:T(128)S(1)}, f32[128]{0:T(128)}, u32[]{:S(2)}) copy-start(f32[128]{0:T(128)} %copy-done.48) | copy-start | bytes 1540
  139.6 35.6 %copy-start.51 = (f32[4]{0:T(128)S(1)}, f32[4]{0:T(128)}, u32[]{:S(2)}) copy-start(f32[4]{0:T(128)} %copy-done.50) | copy-start | bytes 52
  139.6 35.6 %copy-start.53 = (f32[4]{0:T(128)S(1)}, f32[4]{0:T(128)}, u32[]{:S(2)}) copy-start(f32[4]{0:T(128)} %copy-done.52) | copy-start | bytes 52
  139.6 35.6 %copy-start.54 = (f32[4]{0:T(128)S(1)}, f32[4]{0:T(128)}, u32[]{:S(2)}) copy-start(f32[4]{0:T(128)} %get-tuple-element.144) | copy-start | bytes 52
  145.2 15.7 %all-to-all-start.4 = ((bf16[4,512,128]{1,2,0:T(8,128)(2,1)}), bf16[4,512,128]{1,2,0:T(8,128)(2,1)S(1)}, u32[]{:S(2)}, u32[]{:S(2)}) async-start(bf16[4,512,128]{1,2,0:T(8,128)(2,1)} %copy.50), calls=%async_computation.4 | async-start | bytes 1048576 | tf_op jit(solution)/shard_map/all_to_all | solution.py:234
  160.9 18.9 %all-to-all-start.5 = ((bf16[4,512,128]{2,1,0:T(8,128)(2,1)}), bf16[4,512,128]{2,1,0:T(8,128)(2,1)S(1)}, u32[]{:S(2)}, u32[]{:S(2)}) async-start(bf16[4,512,128]{2,1,0:T(8,128)(2,1)} %multiply_convert_fusion), calls=%async_computation.5 | async-start | bytes 1048576 | tf_op jit(solution)/shard_map/all_to_all | solution.py:235
where the time goes:
time: 182 us; the launch traced here: 181 us
  blocking collectives  46 us (25%)
  waiting for transfers between devices  40.6 us (22%)
  starting transfers between devices  25.1 us (14%)
  local copies, waits for them, and re-layouts  23 us (13%)
  other arithmetic  21.8 us (12%)
  matrix products  20.4 us (11%)
  between operations  3.64 us (2%)
    psum x1, blocking collectives, shards(): summed = lax.psum(partial_value, 'seq')  16.8 us
    all_to_all x1, waiting for transfers between devices, shards(): lax.all_to_all(widen(k_proj[0]), 'seq', split_axis=1, concat_axis=0, tile...  12.7 us
    all_to_all x1, waiting for transfers between devices, shards(): lax.all_to_all(k_terms.reshape(flat_shape), 'seq', split_axis=0, concat_a...  11.1 us
    unnamed x120, local copies, waits for them, and re-layouts  10.3 us
    all_to_all x1, waiting for transfers between devices, shards(): lax.all_to_all(q_proj[0], 'seq', split_axis=1, concat_axis=0, tiled=True)  9.79 us
    unnamed x1, blocking collectives  8.26 us
    all_to_all x1, starting transfers between devices, shards(): lax.all_to_all(widen(k_proj[0]), 'seq', split_axis=1, concat_axis=0, tile...  6.32 us
    dot_general x4, matrix products, shards(): jnp.einsum('htu,thd->uhd', grad_logits, q_block[index * block_rows:ending...  5.53 us
  transfers between devices with their start and end apart: 6, of which 5 were waited for; matrix products, arithmetic and copies ran while one was open for 15% of the time, Pallas kernels for 0%

commit v1 on v0

v1 whole, which is shorter than its diff:
```python
import functools
import math

import jax
import jax.numpy as jnp
from jax import lax
from jax.experimental import pallas as pl
from jax.experimental.pallas import tpu as pltpu
from jax.sharding import PartitionSpec as P

HD = 128
LOGIT_DIVISOR = 0.05
INV_ROOT = 1.0 / math.sqrt(HD)
EXP2_SCALE = INV_ROOT * math.log2(math.e)
F32 = jnp.float32
BF16 = jnp.bfloat16
HIGHEST = lax.Precision.HIGHEST
NT = (((1,), (1,)), ((), ()))
TN = (((0,), (0,)), ((), ()))
NN = (((1,), (0,)), ((), ()))


def dot(a, b, dims, precision=None):
    return lax.dot_general(a, b, dims, precision=precision, preferred_element_type=F32)


def rms_scale(wide):
    return lax.rsqrt(jnp.mean(wide * wide, axis=-1, keepdims=True) + 1e-06)


def normed(source, gain):
    wide = source.astype(F32)
    return (wide * rms_scale(wide) * gain).astype(BF16)


def norm_back(source, gain, grad_out):
    wide = source.astype(F32)
    inv_rms = rms_scale(wide)
    scaled = gain * grad_out
    return (
        inv_rms * scaled - wide * inv_rms**3 * jnp.mean(scaled * wide, axis=-1, keepdims=True)
    ).astype(BF16)


def split_rows(row, rows=16):
    high = row.astype(BF16).astype(F32)
    low = row - high
    index = lax.broadcasted_iota(jnp.int32, (rows, row.shape[1]), 0)
    return jnp.where(index == 0, high, jnp.where(index == 1, low, 0.0)).astype(BF16)


def pad_rows(rows):
    missing = -rows.shape[0] % 8
    if missing:
        rows = jnp.concatenate([rows, jnp.zeros((missing, rows.shape[1]), F32)], axis=0)
    return rows


def loop(count, body):
    if isinstance(count, int) and count <= 4:
        for i in range(count):
            body(i)
    else:
        lax.fori_loop(0, count, lambda i, c: (body(i), c)[1], 0)


def kernel(
    cfg, q_ref, k_ref, v_ref, qg_ref, kg_ref, w_ref, len_ref, qe_ref, te_ref,
    qo_ref, ko_ref, vo_ref, wg_ref, rl_ref, cl_ref,
    qu, kall, pall, rs, coef, cwp, cwr, pps, ppr, sums, gps, vds, dkp, dkr, dqt, qea, tea,
    k_send, k_recv, c_send, c_recv, p_send, p_recv, s_send, s_recv, g_send, g_recv,
    v_send, v_recv, d_send, d_recv, e_send, e_recv, t_send, t_recv,
):
    n, nb, nr, tok, heads, kv, width, qb = cfg
    gqa = heads // kv
    npass = nb * nr
    total_q = nb * qb
    peers = n * npass
    s, b, r = lax.axis_index("seq"), lax.axis_index("blk"), lax.axis_index("rep")
    me_p = b * nr + r
    me = s * npass + me_p

    def coords(o):
        peer = lax.rem(me + o, peers)
        ps = peer // npass
        pp = lax.rem(peer, npass)
        return ps, pp, {"seq": ps, "blk": pp // nr, "rep": lax.rem(pp, nr)}

    def lanes(i):
        if isinstance(i, int):
            return slice(i * HD, (i + 1) * HD)
        return pl.ds(pl.multiple_of(i * HD, HD), HD)

    barrier = pltpu.get_barrier_semaphore()

    def greet(i):
        pl.semaphore_signal(
            barrier, inc=1, device_id=coords(i + 1)[2], device_id_type=pl.DeviceIdType.MESH
        )

    lax.fori_loop(0, peers - 1, lambda i, c: (greet(i), c)[1], 0)

    kg = kg_ref[...]
    qg = qg_ref[...]
    for g in range(kv):
        kall[s, g] = normed(k_ref[:, g * HD : (g + 1) * HD], kg)
    pl.semaphore_wait(barrier, peers - 1)

    def remote(src, dst, send, recv, device):
        return pltpu.make_async_remote_copy(
            src_ref=src, dst_ref=dst, send_sem=send, recv_sem=recv,
            device_id=device, device_id_type=pl.DeviceIdType.MESH,
        )

    def k_copy(dst, src):
        return remote(kall.at[src], kall.at[src], k_send.at[dst], k_recv.at[src], {"seq": dst})

    def c_copy(dst, src):
        return remote(cwp.at[dst], cwr.at[src], c_send.at[dst], c_recv.at[src], {"seq": dst})

    def d_copy(dst, src):
        return remote(dkp.at[dst], dkr.at[src], d_send.at[dst], d_recv.at[src], {"seq": dst})

    def v_copy(dst, src):
        return remote(vds.at[src], vds.at[src], v_send.at[dst], v_recv.at[src], {"seq": dst})

    def s_copy(dst, src):
        return remote(sums.at[src], sums.at[src], s_send.at[dst], s_recv.at[src], {"seq": dst})

    def g_copy(dst, src):
        return remote(gps.at[src], gps.at[src], g_send.at[dst], g_recv.at[src], {"seq": dst})

    def e_copy(dst, src):
        return remote(qe_ref, qea.at[src], e_send.at[dst], e_recv.at[src], {"blk": dst})

    def t_copy(dst, src):
        return remote(te_ref, tea.at[src], t_send.at[dst], t_recv.at[src], {"blk": dst})

    def p_copy(o, slot_s, slot_p, device, dst_head, index):
        return remote(
            pps.at[dst_head], ppr.at[slot_s, slot_p], p_send.at[index],
            p_recv.at[slot_s, slot_p], device,
        )

    def fori(lo, hi, body):
        lax.fori_loop(lo, hi, lambda i, c: (body(i), c)[1], 0)

    later = n - 1 - s
    fori(0, later, lambda i: k_copy(n - 1 - i, s).start())

    def other_blk(i):
        return lax.rem(b + 1 + i, nb)

    def other_seq(i):
        return lax.rem(s + 1 + i, n)

    for i in range(nb - 1):
        t_copy(other_blk(i), b).start()
        e_copy(other_blk(i), b).start()

    def q_norm(h):
        qu[h] = normed(q_ref[:, lanes(h)], qg)

    loop(heads, q_norm)

    def forward(j, diagonal):
        def one(h):
            logits = dot(kall[j, h // gqa], qu[h], NT)
            powers = jnp.exp2(logits * EXP2_SCALE)
            if diagonal:
                u = lax.broadcasted_iota(jnp.int32, powers.shape, 0)
                t = lax.broadcasted_iota(jnp.int32, powers.shape, 1)
                powers = jnp.where(u <= t, powers, 0.0)
            pall[j, h] = powers.astype(BF16)
            row = jnp.sum(powers, axis=0, keepdims=True)
            rs[h] = row if diagonal else rs[h] + row

        loop(heads, one)

    forward(s, True)

    def unit_queries(rows):
        wide = rows.astype(F32)
        return (
            wide * lax.rsqrt(jnp.sum(wide * wide, axis=1, keepdims=True) + 1e-06)
        ).astype(BF16)

    qea[b] = unit_queries(qe_ref[...])
    tea[b] = te_ref[...]

    def forward_step(i):
        j = s - 1 - i
        k_copy(s, j).wait_recv()
        forward(j, False)

    fori(0, s, forward_step)

    length = len_ref[0, 0]
    position = s * tok + lax.broadcasted_iota(jnp.int32, (1, tok), 1)
    live = jnp.where(position < length, 1.0, 0.0) / jnp.full((1, tok), length, jnp.int32).astype(F32)

    def weigh(h):
        coef[h] = live / rs[h]

    loop(heads, weigh)

    def column_step(i):
        def one(h):
            both = dot(split_rows(coef[h]), pall[i, h], NT)
            cwp[i, pl.ds(h, 1), :] = both[0:1] + both[1:2]

        loop(heads, one)

        @pl.when(i < s)
        def _():
            c_copy(i, s).start()

    fori(0, s + 1, column_step)

    def query_step(i):
        src = lax.rem(b + 1 + i, nb)
        t_copy(b, src).wait_recv()
        e_copy(b, src).wait_recv()
        qea[src] = unit_queries(qea[src])

    for i in range(nb - 1):
        query_step(i)

    cwr[s] = cwp[s]

    def column_add(i):
        src = s + 1 + i
        c_copy(s, src).wait_recv()
        cwr[s] = cwr[s] + cwr[src]

    fori(0, later, column_add)
    col_weight = cwr[s]
    for g in range(kv):
        part = dot(
            col_weight[g * gqa : (g + 1) * gqa],
            v_ref[:, g * HD : (g + 1) * HD].astype(F32), NN, HIGHEST,
        )
        for i in range(gqa):
            pps[g * gqa + i] = jnp.broadcast_to(part[i : i + 1], (8, HD))

    def p_start(i):
        ps, _, device = coords(i + 1)
        p_copy(i, s, me_p, device, ps, i).start()

    fori(0, peers - 1, p_start)
    ppr[s, me_p] = pps[s]

    def p_wait(i):
        ps, pp, device = coords(i + 1)
        p_copy(i, ps, pp, device, ps, i).wait_recv()

    fori(0, peers - 1, p_wait)
    rows = []
    for p in range(npass):
        row = ppr[0, p]
        for i in range(1, n):
            row = row + ppr[i, p]
        rows.append(row[0:1])
    pooled = jnp.concatenate(rows, axis=0).astype(BF16).astype(F32)
    part = dot(pooled.astype(BF16), w_ref[...], NN)
    fold = sums.shape[1] // npass
    fw = width // fold
    sums[s] = jnp.concatenate(
        [part[:, i * fw : (i + 1) * fw] for i in range(fold)], axis=0
    ).astype(BF16)
    fori(0, n - 1, lambda i: s_copy(other_seq(i), s).start())
    fori(0, n - 1, lambda i: s_copy(s, other_seq(i)).wait_recv())
    stacked = sums[0].astype(F32)
    for i in range(1, n):
        stacked = stacked + sums[i].astype(F32)
    summed = jnp.concatenate(
        [stacked[i * npass : (i + 1) * npass] for i in range(fold)], axis=1
    )

    inv_norm = lax.rsqrt(jnp.sum(summed * summed, axis=1, keepdims=True) + 1e-06)
    unit = summed * inv_norm
    emb = unit.astype(BF16)
    blocks = range(nb)
    score = [dot(emb, qea[i], NT) / LOGIT_DIVISOR for i in blocks]
    teach = [tea[i] for i in blocks]
    es = [jnp.exp(x) for x in score]
    et = [jnp.exp(x) for x in teach]
    gap = [et[i] * (teach[i] - score[i]) for i in blocks]
    zs = [jnp.sum(x, axis=0, keepdims=True) for x in es]
    zt = [jnp.sum(x, axis=0, keepdims=True) for x in et]
    cs = sum(jnp.sum(x, axis=1, keepdims=True) for x in es)
    ct = sum(jnp.sum(x, axis=1, keepdims=True) for x in et)
    cg = sum(jnp.sum(x, axis=1, keepdims=True) for x in gap)
    grad_emb = jnp.zeros((npass, width), F32)
    for i in blocks:
        ds = (es[i] / zs[i] - et[i] / zt[i]) / total_q + (es[i] / cs - et[i] / ct) / npass
        grad_emb = grad_emb + dot(ds.astype(BF16), qea[i], NN)
    grad_emb = grad_emb / LOGIT_DIVISOR
    grad_sum = (
        (grad_emb - unit * jnp.sum(unit * grad_emb, axis=1, keepdims=True)) * inv_norm
    ).astype(BF16)
    grad_pool = dot(grad_sum, w_ref[...], NT)
    index = lax.broadcasted_iota(jnp.int32, grad_pool.shape, 0)
    mine = jnp.sum(jnp.where(index == me_p, grad_pool, 0.0), axis=0, keepdims=True)
    gps[s] = jnp.broadcast_to(mine, (8, HD))
    fori(0, n - 1, lambda i: g_copy(other_seq(i), s).start())

    cl_ref[...] = cg / ct - jnp.log(ct) + jnp.log(cs)
    for i in blocks:

        @pl.when(b == i)
        def _():
            rl_ref[...] = (
                jnp.sum(gap[i], axis=0, keepdims=True) / zt[i] - jnp.log(zt[i]) + jnp.log(zs[i])
            )

    fori(0, n - 1, lambda i: g_copy(s, other_seq(i)).wait_recv())
    pool_grads = jnp.concatenate([gps[h, 0:1, :] for h in range(heads)], axis=0)
    for g in range(kv):
        vds[s, g * gqa : (g + 1) * gqa] = dot(
            pool_grads[g * gqa : (g + 1) * gqa],
            v_ref[:, g * HD : (g + 1) * HD].astype(F32), NT, HIGHEST,
        )
    fori(0, later, lambda i: v_copy(n - 1 - i, s).start())

    wg_ref[...] = dot(
        pad_rows(pooled).T.astype(BF16), pad_rows(grad_sum.astype(F32)).astype(BF16), NN
    ).astype(BF16)
    col_rounded = col_weight.astype(BF16).astype(F32)
    for g in range(kv):
        vo_ref[:, g * HD : (g + 1) * HD] = dot(
            pad_rows(col_rounded[g * gqa : (g + 1) * gqa]).T,
            pad_rows(pool_grads[g * gqa : (g + 1) * gqa]), NN, HIGHEST,
        ).astype(BF16)

    fori(0, s, lambda i: v_copy(s, i).wait_recv())

    def mean_head(h):
        def add(j, carry):
            both = dot(split_rows(vds[j, pl.ds(h, 1), :]), pall[j, h], NN)
            return carry + both[0:1] + both[1:2]

        rs[h] = lax.fori_loop(0, s + 1, add, jnp.zeros((1, tok), F32)) / rs[h]
        dqt[h] = jnp.zeros((HD, tok), F32)

    loop(heads, mean_head)

    def backward_step(j):
        def one_kv(g):
            columns = pad_rows(vds[j, pl.ds(g * gqa, gqa), :]).T
            total = jnp.zeros((tok, HD), F32)
            for i in range(gqa):
                h = g * gqa + i
                grad_logits = (
                    pall[j, h].astype(F32)
                    * (coef[h] * INV_ROOT)
                    * (columns[:, i : i + 1] - rs[h])
                ).astype(BF16)
                total = total + dot(grad_logits, qu[h], NN)
                dqt[h] = dqt[h] + dot(kall[j, g], grad_logits, TN)
            dkp[j, g] = total.astype(BF16)

        loop(kv, one_kv)

        @pl.when(j < s)
        def _():
            d_copy(j, s).start()

    fori(0, s + 1, backward_step)

    def q_out(h):
        qo_ref[:, lanes(h)] = norm_back(q_ref[:, lanes(h)], qg, dqt[h].T)

    loop(heads, q_out)

    fori(0, later, lambda i: d_copy(s, s + 1 + i).wait_recv())
    for g in range(kv):
        total = lax.fori_loop(
            0, later, lambda i, c: c + dkr[s + 1 + i, g].astype(F32), dkp[s, g].astype(F32)
        )
        ko_ref[:, g * HD : (g + 1) * HD] = norm_back(k_ref[:, g * HD : (g + 1) * HD], kg, total)

    fori(0, later, lambda i: k_copy(n - 1 - i, s).wait_send())
    fori(0, later, lambda i: v_copy(n - 1 - i, s).wait_send())
    for i in range(nb - 1):
        t_copy(other_blk(i), b).wait_send()
        e_copy(other_blk(i), b).wait_send()
    fori(0, s, lambda i: c_copy(i, s).wait_send())
    fori(0, s, lambda i: d_copy(i, s).wait_send())
    fori(0, n - 1, lambda i: s_copy(other_seq(i), s).wait_send())
    fori(0, n - 1, lambda i: g_copy(other_seq(i), s).wait_send())

    def p_done(i):
        ps, _, device = coords(i + 1)
        p_copy(i, s, me_p, device, ps, i).wait_send()

    fori(0, peers - 1, p_done)


def shards(q_proj, k_proj, v_proj, q_gain, k_gain, out_weight, lengths, query_emb, teacher):
    n, nb, nr = lax.axis_size("seq"), lax.axis_size("blk"), lax.axis_size("rep")
    tok = q_proj.shape[1]
    heads = q_proj.shape[2] // HD
    kv = k_proj.shape[2] // HD
    width = out_weight.shape[1]
    qb = query_emb.shape[0]
    npass = nb * nr
    assert out_weight.shape[0] == HD and heads == n and teacher.shape[1] == npass
    peers = n * npass
    fold = 4
    vmem = pl.BlockSpec(memory_space=pltpu.VMEM)
    smem = pl.BlockSpec(memory_space=pltpu.SMEM)
    sem = pltpu.SemaphoreType.DMA
    cfg = (n, nb, nr, tok, heads, kv, width, qb)
    outs = pl.pallas_call(
        functools.partial(kernel, cfg),
        out_shape=(
            jax.ShapeDtypeStruct((tok, heads * HD), BF16),
            jax.ShapeDtypeStruct((tok, kv * HD), BF16),
            jax.ShapeDtypeStruct((tok, kv * HD), BF16),
            jax.ShapeDtypeStruct((HD, width), BF16),
            jax.ShapeDtypeStruct((1, qb), F32),
            jax.ShapeDtypeStruct((npass, 1), F32),
        ),
        in_specs=[vmem] * 6 + [smem] + [vmem] * 2,
        out_specs=(vmem,) * 6,
        scratch_shapes=[
            pltpu.VMEM((heads, tok, HD), BF16),
            pltpu.VMEM((n, kv, tok, HD), BF16),
            pltpu.VMEM((n, heads, tok, tok), BF16),
            pltpu.VMEM((heads, 1, tok), F32),
            pltpu.VMEM((heads, 1, tok), F32),
            pltpu.VMEM((n, heads, tok), F32),
            pltpu.VMEM((n, heads, tok), F32),
            pltpu.VMEM((heads, 8, HD), F32),
            pltpu.VMEM((n, npass, 8, HD), F32),
            pltpu.VMEM((n, npass * fold, width // fold), BF16),
            pltpu.VMEM((n, 8, HD), F32),
            pltpu.VMEM((n, heads, tok), F32),
            pltpu.VMEM((n, kv, tok, HD), BF16),
            pltpu.VMEM((n, kv, tok, HD), BF16),
            pltpu.VMEM((heads, HD, tok), F32),
            pltpu.VMEM((nb, qb, width), BF16),
            pltpu.VMEM((nb, npass, qb), F32),
            sem((n,)), sem((n,)), sem((n,)), sem((n,)),
            sem((peers,)), sem((n, npass)),
            sem((n,)), sem((n,)), sem((n,)), sem((n,)),
            sem((n,)), sem((n,)), sem((n,)), sem((n,)),
            sem((nb,)), sem((nb,)), sem((nb,)), sem((nb,)),
        ],
        compiler_params=pltpu.CompilerParams(
            collective_id=0, has_side_effects=True, vmem_limit_bytes=58 * 2**20
        ),
    )(
        q_proj[0], k_proj[0], v_proj[0], q_gain[None], k_gain[None], out_weight, lengths,
        query_emb, teacher.T,
    )
    q_grad, k_grad, v_grad, weight_grad, row_loss, col_loss = outs
    return q_grad[None], k_grad[None], v_grad[None], weight_grad, row_loss[0], col_loss[:, 0]


def solution(mesh):
    placed = (
        P(("grp", "blk", "rep"), "seq", None),
        P(("grp", "blk", "rep"), "seq", None),
        P(("grp", "blk", "rep"), "seq", None),
        P(),
        P(),
        P("seq", None),
        P(("grp", "blk", "rep"), None),
        P(("grp", "blk"), None),
        P(("grp", "blk"), None),
    )
    return jax.shard_map(
        shards,
        mesh=mesh,
        in_specs=placed,
        out_specs=(
            P(("grp", "blk", "rep"), "seq", None),
            P(("grp", "blk", "rep"), "seq", None),
            P(("grp", "blk", "rep"), "seq", None),
            P(("grp", "seq"), None),
            P(("grp", "blk")),
            P("grp"),
        ),
        check_vma=False,
    )
```

time: 182 us -> 65.6 us (0.36)
  Pallas kernels: 0 us -> 57.9 us
  blocking collectives: 46 us -> 0 us
  waiting for transfers between devices: 40.6 us -> 0 us
  starting transfers between devices: 25.1 us -> 0 us
  other arithmetic: 21.8 us -> 0.63 us
  matrix products: 20.4 us -> 0 us
  local copies, waits for them, and re-layouts: 23 us -> 5.56 us
  between operations: 3.64 us -> 1.3 us
    pallas_call x0 -> x1, Pallas kernels: none -> 57.9 us  [shards(): pl.pallas_call(functools.partial(kernel, cfg), out_shape=(jax.ShapeDtypeS...]
    all_to_all x6 -> x0, waiting for transfers between devices: 40.6 us -> none  [the longest x1 12.7 us: shards(): lax.all_to_all(widen(k_proj[0]), 'seq', split_axis=1, concat_axis=0, tile...]
    all_to_all x6 -> x0, starting transfers between devices: 25.1 us -> none  [the longest x1 6.32 us: shards(): lax.all_to_all(widen(k_proj[0]), 'seq', split_axis=1, concat_axis=0, tile...]
    psum x2 -> x0, blocking collectives: 22.3 us -> none  [the longest x1 16.8 us: shards(): summed = lax.psum(partial_value, 'seq')]
    dot_general x21 -> x0, matrix products: 20.4 us -> none  [the longest x4 5.53 us: shards(): jnp.einsum('htu,thd->uhd', grad_logits, q_block[index * block_rows:ending...]
    all_gather x3 -> x0, blocking collectives: 15.5 us -> none  [the longest x1 5.22 us: shards(): lax.all_gather(passage_unit.astype(jnp.bfloat16), ('blk', 'rep'), axis=0,...]
    unnamed x1 -> x0, blocking collectives: 8.26 us -> none
    reduce_sum x14 -> x0, other arithmetic: 7.84 us -> none  [the longest x1 1.61 us: norm_back(): jnp.mean(scaled_grad * wide, axis=-1, keepdims=True)]
  transfers between devices with their start and end apart: 6 -> 0, of which waited for: 5 -> 0; matrix products, arithmetic and copies ran while one was open for 15% -> 0% of each run, Pallas kernels for 0% -> 0%
where the time goes in v1:
time: 65.6 us; the launch traced here: 65.4 us
  Pallas kernels  57.9 us (88%)
  local copies, waits for them, and re-layouts  5.56 us (8%)
  between operations  1.3 us (2%)
    pallas_call x1, Pallas kernels, shards(): pl.pallas_call(functools.partial(kernel, cfg), out_shape=(jax.ShapeDtypeS...  57.9 us
    unnamed x15, local copies, waits for them, and re-layouts  5.56 us

profile of v1, /device:TPU:0, one launch (start us, length us, event | category | flops | bytes accessed | tf_op | source)
XLA Modules:
  0.0 65.4 jit_solution(10322378760960035733)
XLA Ops:
  1.3 57.9 %shard_map.136 = (bf16[512,512]{1,0:T(8,128)(2,1)}, bf16[512,128]{1,0:T(8,128)(2,1)}, bf16[512,128]{1,0:T(8,128)(2,1)}, bf16[128,2560]{1,0:T(8,128)(2,1)}, f32[1,128]{1,0:T(1,128)}, /*index=5*/f32[4,1]{1,0:T(4,128)}) custom-call(bf16[512,512]{1,0:T(8,128)(2,1)} %bitcast.10, bf16[512,128]{1,0:T(8,128)(2,1)} %bitcast.12, bf16[512,128]{1,0:T(8,128)(2,1)} %bitcast.13, ...), custom_call_target="tpu_custom_call" | custom-call | tf_op jit(solution)/shard_map/pallas_call | solution.py:415
  59.2 0.0 copy-start.3
  59.2 0.7 %copy-done.3 = f32[4,1]{1,0:T(4,128)S(1)} copy-done((f32[4,1]{1,0:T(4,128)S(1)}, f32[4,1]{1,0:T(4,128)}, u32[]{:S(2)}) %copy-start.3) | copy-done | bytes 40
  59.9 0.6 reduce
  60.5 0.0 copy-start.2
  60.5 0.0 copy-start
  60.5 1.9 %copy.21 = bf16[1,512,512]{2,1,0:T(8,128)(2,1)} copy(bf16[1,512,512]{2,1,0:T(8,128)(2,1)} %bitcast.11) | data formatting | bytes 1048576
  62.5 0.0 copy-done.2
  62.5 0.0 copy-start.1
  62.5 0.7 %copy.22 = bf16[1,512,128]{2,1,0:T(8,128)(2,1)} copy(bf16[1,512,128]{2,1,0:T(8,128)(2,1)S(1)} %bitcast.15) | data formatting | bytes 262144
  63.1 0.3 copy-done.1
  63.4 0.7 %copy.23 = bf16[1,512,128]{2,1,0:T(8,128)(2,1)} copy(bf16[1,512,128]{2,1,0:T(8,128)(2,1)S(1)} %bitcast.14) | data formatting | bytes 262144
  64.1 0.0 copy-done
  64.1 0.0 copy-start.4
  64.1 0.8 %copy.24 = bf16[128,2560]{1,0:T(8,128)(2,1)} copy(bf16[128,2560]{1,0:T(8,128)(2,1)S(1)} %copy-done) | data formatting | bytes 1310720
  64.9 0.0 copy-done.4
  64.9 0.5 copy.25
Async XLA Ops:
  59.2 0.7 %copy-start.3 = (f32[4,1]{1,0:T(4,128)S(1)}, f32[4,1]{1,0:T(4,128)}, u32[]{:S(2)}) copy-start(f32[4,1]{1,0:T(4,128)} %get-tuple-element.17) | copy-start | bytes 52
  60.5 1.9 %copy-start.2 = (bf16[512,128]{1,0:T(8,128)(2,1)S(1)}, bf16[512,128]{1,0:T(8,128)(2,1)}, u32[]{:S(2)}) copy-start(bf16[512,128]{1,0:T(8,128)(2,1)} %get-tuple-element.13) | copy-start | bytes 393220
  60.5 3.6 %copy-start = (bf16[128,2560]{1,0:T(8,128)(2,1)S(1)}, bf16[128,2560]{1,0:T(8,128)(2,1)}, u32[]{:S(2)}) copy-start(bf16[128,2560]{1,0:T(8,128)(2,1)} %get-tuple-element.27) | copy-start | bytes 1966084
  62.5 1.0 %copy-start.1 = (bf16[512,128]{1,0:T(8,128)(2,1)S(1)}, bf16[512,128]{1,0:T(8,128)(2,1)}, u32[]{:S(2)}) copy-start(bf16[512,128]{1,0:T(8,128)(2,1)} %get-tuple-element.14) | copy-start | bytes 393220
  64.1 0.8 %copy-start.4 = (f32[1,128]{1,0:T(1,128)S(1)}, f32[1,128]{1,0:T(1,128)}, u32[]{:S(2)}) copy-start(f32[1,128]{1,0:T(1,128)} %get-tuple-element.16) | copy-start | bytes 1540

commit v2 on v1

--- a/solution.py
+++ b/solution.py
@@ -65,9 +65,10 @@
 
 
 def kernel(
-    cfg, q_ref, k_ref, v_ref, qg_ref, kg_ref, w_ref, len_ref, qe_ref, te_ref,
-    qo_ref, ko_ref, vo_ref, wg_ref, rl_ref, cl_ref,
-    qu, kall, pall, rs, coef, cwp, cwr, pps, ppr, sums, gps, vds, dkp, dkr, dqt, qea, tea,
+    cfg, q_hbm, k_hbm, v_hbm, qg_ref, kg_ref, w_hbm, len_ref, qe_hbm, te_ref,
+    qo_hbm, ko_hbm, vo_hbm, wg_hbm, rl_ref, cl_ref,
+    q_ref, k_ref, v_ref, w_ref, qo_ref, ko_ref, vo_ref, wg_ref, in_sem, out_sem, qer, h_send, f_send,
+    qu, kall, pall, rs, coef, cwp, cwr, pps, ppr, sums, gps, vds, dkp, dkr, dkf, dqt, qea, tea,
     k_send, k_recv, c_send, c_recv, p_send, p_recv, s_send, s_recv, g_send, g_recv,
     v_send, v_recv, d_send, d_recv, e_send, e_recv, t_send, t_recv,
 ):
@@ -91,6 +92,9 @@
             return slice(i * HD, (i + 1) * HD)
         return pl.ds(pl.multiple_of(i * HD, HD), HD)
 
+    def fori(lo, hi, body):
+        lax.fori_loop(lo, hi, lambda i, c: (body(i), c)[1], 0)
+
     barrier = pltpu.get_barrier_semaphore()
 
     def greet(i):
@@ -100,10 +104,32 @@
 
     lax.fori_loop(0, peers - 1, lambda i, c: (greet(i), c)[1], 0)
 
+    loads = [
+        pltpu.make_async_copy(src, dst, in_sem.at[i])
+        for i, (src, dst) in enumerate([
+            (k_hbm, k_ref), (q_hbm, q_ref), (qe_hbm, qer.at[b]), (v_hbm, v_ref), (w_hbm, w_ref)
+        ])
+    ]
+    for load in loads:
+        load.start()
+    stores = [
+        pltpu.make_async_copy(src, dst, out_sem.at[i])
+        for i, (src, dst) in enumerate([
+            (qo_ref, qo_hbm), (ko_ref, ko_hbm), (vo_ref, vo_hbm), (wg_ref, wg_hbm)
+        ])
+    ]
     kg = kg_ref[...]
     qg = qg_ref[...]
+    loads[0].wait()
     for g in range(kv):
         kall[s, g] = normed(k_ref[:, g * HD : (g + 1) * HD], kg)
+    loads[1].wait()
+
+    def q_norm(h):
+        qu[h] = normed(q_ref[:, lanes(h)], qg)
+
+    loop(heads, q_norm)
+    loads[2].wait()
     pl.semaphore_wait(barrier, peers - 1)
 
     def remote(src, dst, send, recv, device):
@@ -112,8 +138,29 @@
             device_id=device, device_id_type=pl.DeviceIdType.MESH,
         )
 
-    def k_copy(dst, src):
-        return remote(kall.at[src], kall.at[src], k_send.at[dst], k_recv.at[src], {"seq": dst})
+    even = lax.rem(s, 2) == 0
+    partner = s + 1 - 2 * lax.rem(s, 2)
+
+    def k_copy(dst, j):
+        return remote(kall.at[j], kall.at[j], k_send.at[dst], k_recv.at[j], {"seq": dst})
+
+    def k_pass(j):
+        return remote(kall.at[j], kall.at[j], f_send.at[j], k_recv.at[j], {"seq": partner})
+
+    def k_wait(j):
+        k_copy(s, j).wait_recv()
+
+    evens = (n - 1 - s) // 2
+
+    def even_after(i):
+        return n - 2 - 2 * i
+
+    def k_start():
+        fori(0, evens, lambda i: k_copy(even_after(i), s).start())
+
+        @pl.when(even)
+        def _():
+            k_pass(s).start()
 
     def c_copy(dst, src):
         return remote(cwp.at[dst], cwr.at[src], c_send.at[dst], c_recv.at[src], {"seq": dst})
@@ -130,8 +177,28 @@
     def g_copy(dst, src):
         return remote(gps.at[src], gps.at[src], g_send.at[dst], g_recv.at[src], {"seq": dst})
 
+    half = qb // nr
+
     def e_copy(dst, src):
-        return remote(qe_ref, qea.at[src], e_send.at[dst], e_recv.at[src], {"blk": dst})
+        part = pl.ds(pl.multiple_of(r * half, half), half)
+        return remote(
+            qer.at[b, part], qer.at[src, part], e_send.at[dst], e_recv.at[src, r], {"blk": dst}
+        )
+
+    def h_copy(src, i):
+        part = pl.ds(pl.multiple_of(r * half, half), half)
+        return remote(
+            qer.at[src, part], qer.at[src, part], h_send.at[src, i], e_recv.at[src, r],
+            {"rep": lax.rem(r + 1 + i, nr)},
+        )
+
+    def h_wait(src, i):
+        other = lax.rem(r + 1 + i, nr)
+        part = pl.ds(pl.multiple_of(other * half, half), half)
+        remote(
+            qer.at[src, part], qer.at[src, part], h_send.at[src, i], e_recv.at[src, other],
+            {"rep": other},
+        ).wait_recv()
 
     def t_copy(dst, src):
         return remote(te_ref, tea.at[src], t_send.at[dst], t_recv.at[src], {"blk": dst})
@@ -142,11 +209,8 @@
             p_recv.at[slot_s, slot_p], device,
         )
 
-    def fori(lo, hi, body):
-        lax.fori_loop(lo, hi, lambda i, c: (body(i), c)[1], 0)
-
     later = n - 1 - s
-    fori(0, later, lambda i: k_copy(n - 1 - i, s).start())
+    k_start()
 
     def other_blk(i):
         return lax.rem(b + 1 + i, nb)
@@ -157,11 +221,6 @@
     for i in range(nb - 1):
         t_copy(other_blk(i), b).start()
         e_copy(other_blk(i), b).start()
-
-    def q_norm(h):
-        qu[h] = normed(q_ref[:, lanes(h)], qg)
-
-    loop(heads, q_norm)
 
     def forward(j, diagonal):
         def one(h):
@@ -185,15 +244,26 @@
             wide * lax.rsqrt(jnp.sum(wide * wide, axis=1, keepdims=True) + 1e-06)
         ).astype(BF16)
 
-    qea[b] = unit_queries(qe_ref[...])
+    qea[b] = unit_queries(qer[b])
     tea[b] = te_ref[...]
 
     def forward_step(i):
         j = s - 1 - i
-        k_copy(s, j).wait_recv()
+        k_wait(j)
+
+        @pl.when(even)
+        def _():
+            k_pass(j).start()
+
         forward(j, False)
 
     fori(0, s, forward_step)
+
+    for i in range(nb - 1):
+        src = other_blk(i)
+        e_copy(b, src).wait_recv()
+        for o in range(nr - 1):
+            h_copy(src, o).start()
 
     length = len_ref[0, 0]
     position = s * tok + lax.broadcasted_iota(jnp.int32, (1, tok), 1)
@@ -220,8 +290,9 @@
     def query_step(i):
         src = lax.rem(b + 1 + i, nb)
         t_copy(b, src).wait_recv()
-        e_copy(b, src).wait_recv()
-        qea[src] = unit_queries(qea[src])
+        for o in range(nr - 1):
+            h_wait(src, o)
+        qea[src] = unit_queries(qer[src])
 
     for i in range(nb - 1):
         query_step(i)
@@ -235,6 +306,7 @@
 
     fori(0, later, column_add)
     col_weight = cwr[s]
+    loads[3].wait()
     for g in range(kv):
         part = dot(
             col_weight[g * gqa : (g + 1) * gqa],
@@ -261,6 +333,7 @@
         for i in range(1, n):
             row = row + ppr[i, p]
         rows.append(row[0:1])
+    loads[4].wait()
     pooled = jnp.concatenate(rows, axis=0).astype(BF16).astype(F32)
     part = dot(pooled.astype(BF16), w_ref[...], NN)
     fold = sums.shape[1] // npass
@@ -305,7 +378,11 @@
     gps[s] = jnp.broadcast_to(mine, (8, HD))
     fori(0, n - 1, lambda i: g_copy(other_seq(i), s).start())
 
-    cl_ref[...] = cg / ct - jnp.log(ct) + jnp.log(cs)
+    col_loss = cg / ct - jnp.log(ct) + jnp.log(cs)
+    square = [lax.broadcasted_iota(jnp.int32, (npass, npass), i) for i in range(2)]
+    cl_ref[...] = jnp.sum(
+        jnp.where(square[0] == square[1], col_loss, 0.0), axis=0, keepdims=True
+    )
     for i in blocks:
 
         @pl.when(b == i)
@@ -332,6 +409,9 @@
             pad_rows(col_rounded[g * gqa : (g + 1) * gqa]).T,
             pad_rows(pool_grads[g * gqa : (g + 1) * gqa]), NN, HIGHEST,
         ).astype(BF16)
+
+    stores[3].start()
+    stores[2].start()
 
     fori(0, s, lambda i: v_copy(s, i).wait_recv())
 
@@ -358,33 +438,50 @@
                 ).astype(BF16)
                 total = total + dot(grad_logits, qu[h], NN)
                 dqt[h] = dqt[h] + dot(kall[j, g], grad_logits, TN)
-            dkp[j, g] = total.astype(BF16)
+            dkf[g] = total
 
         loop(kv, one_kv)
 
-        @pl.when(j < s)
-        def _():
-            d_copy(j, s).start()
-
-    fori(0, s + 1, backward_step)
+    def send_step(j):
+        backward_step(j)
+
+        for g in range(kv):
+            dkp[j, g] = dkf[g].astype(BF16)
+        d_copy(j, s).start()
+
+    fori(0, s, send_step)
+    backward_step(s)
 
     def q_out(h):
         qo_ref[:, lanes(h)] = norm_back(q_ref[:, lanes(h)], qg, dqt[h].T)
 
     loop(heads, q_out)
-
-    fori(0, later, lambda i: d_copy(s, s + 1 + i).wait_recv())
+    stores[0].start()
+
+    def d_add(i):
+        src = n - 1 - i
+        d_copy(s, src).wait_recv()
+        for g in range(kv):
+            dkf[g] = dkf[g] + dkr[src, g].astype(F32)
+
+    fori(0, later, d_add)
+
     for g in range(kv):
-        total = lax.fori_loop(
-            0, later, lambda i, c: c + dkr[s + 1 + i, g].astype(F32), dkp[s, g].astype(F32)
-        )
-        ko_ref[:, g * HD : (g + 1) * HD] = norm_back(k_ref[:, g * HD : (g + 1) * HD], kg, total)
-
-    fori(0, later, lambda i: k_copy(n - 1 - i, s).wait_send())
+        ko_ref[:, g * HD : (g + 1) * HD] = norm_back(k_ref[:, g * HD : (g + 1) * HD], kg, dkf[g])
+    stores[1].start()
+
+    fori(0, evens, lambda i: k_copy(even_after(i), s).wait_send())
+
+    @pl.when(even)
+    def _():
+        fori(0, s + 1, lambda i: k_pass(i).wait_send())
+
     fori(0, later, lambda i: v_copy(n - 1 - i, s).wait_send())
     for i in range(nb - 1):
         t_copy(other_blk(i), b).wait_send()
         e_copy(other_blk(i), b).wait_send()
+        for o in range(nr - 1):
+            h_copy(other_blk(i), o).wait_send()
     fori(0, s, lambda i: c_copy(i, s).wait_send())
     fori(0, s, lambda i: d_copy(i, s).wait_send())
     fori(0, n - 1, lambda i: s_copy(other_seq(i), s).wait_send())
@@ -395,6 +492,14 @@
         p_copy(i, s, me_p, device, ps, i).wait_send()
 
     fori(0, peers - 1, p_done)
+    for store in stores:
+        store.wait()
+
+
+def finish(*refs):
+    count = len(refs) // 2
+    for i in range(count):
+        refs[count + i][...] = refs[i][...]
 
 
 def shards(q_proj, k_proj, v_proj, q_gain, k_gain, out_weight, lengths, query_emb, teacher):
@@ -405,10 +510,11 @@
     width = out_weight.shape[1]
     qb = query_emb.shape[0]
     npass = nb * nr
-    assert out_weight.shape[0] == HD and heads == n and teacher.shape[1] == npass
+    assert out_weight.shape[0] == HD and heads == n and n % 2 == 0 and teacher.shape[1] == npass
     peers = n * npass
     fold = 4
     vmem = pl.BlockSpec(memory_space=pltpu.VMEM)
+    hbm = pl.BlockSpec(memory_space=pl.ANY)
     smem = pl.BlockSpec(memory_space=pltpu.SMEM)
     sem = pltpu.SemaphoreType.DMA
     cfg = (n, nb, nr, tok, heads, kv, width, qb)
@@ -420,11 +526,22 @@
             jax.ShapeDtypeStruct((tok, kv * HD), BF16),
             jax.ShapeDtypeStruct((HD, width), BF16),
             jax.ShapeDtypeStruct((1, qb), F32),
-            jax.ShapeDtypeStruct((npass, 1), F32),
+            jax.ShapeDtypeStruct((1, npass), F32),
         ),
-        in_specs=[vmem] * 6 + [smem] + [vmem] * 2,
-        out_specs=(vmem,) * 6,
+        in_specs=[hbm] * 3 + [vmem] * 2 + [hbm, smem, hbm, vmem],
+        out_specs=(hbm,) * 4 + (vmem,) * 2,
         scratch_shapes=[
+            pltpu.VMEM((tok, heads * HD), BF16),
+            pltpu.VMEM((tok, kv * HD), BF16),
+            pltpu.VMEM((tok, kv * HD), BF16),
+            pltpu.VMEM((HD, width), BF16),
+            pltpu.VMEM((tok, heads * HD), BF16),
+            pltpu.VMEM((tok, kv * HD), BF16),
+            pltpu.VMEM((tok, kv * HD), BF16),
+            pltpu.VMEM((HD, width), BF16),
+            sem((5,)), sem((4,)),
+            pltpu.VMEM((nb, qb, width), BF16),
+            sem((nb, nr)), sem((n,)),
             pltpu.VMEM((heads, tok, HD), BF16),
             pltpu.VMEM((n, kv, tok, HD), BF16),
             pltpu.VMEM((n, heads, tok, tok), BF16),
@@ -439,6 +556,7 @@
             pltpu.VMEM((n, heads, tok), F32),
             pltpu.VMEM((n, kv, tok, HD), BF16),
             pltpu.VMEM((n, kv, tok, HD), BF16),
+            pltpu.VMEM((kv, tok, HD), F32),
             pltpu.VMEM((heads, HD, tok), F32),
             pltpu.VMEM((nb, qb, width), BF16),
             pltpu.VMEM((nb, npass, qb), F32),
@@ -446,7 +564,7 @@
             sem((peers,)), sem((n, npass)),
             sem((n,)), sem((n,)), sem((n,)), sem((n,)),
             sem((n,)), sem((n,)), sem((n,)), sem((n,)),
-            sem((nb,)), sem((nb,)), sem((nb,)), sem((nb,)),
+            sem((nb,)), sem((nb, nr)), sem((nb,)), sem((nb,)),
         ],
         compiler_params=pltpu.CompilerParams(
             collective_id=0, has_side_effects=True, vmem_limit_bytes=58 * 2**20
@@ -455,8 +573,14 @@
         q_proj[0], k_proj[0], v_proj[0], q_gain[None], k_gain[None], out_weight, lengths,
         query_emb, teacher.T,
     )
+    outs = pl.pallas_call(
+        finish,
+        out_shape=tuple(jax.ShapeDtypeStruct(x.shape, x.dtype) for x in outs),
+        in_specs=[vmem] * len(outs),
+        out_specs=(vmem,) * len(outs),
+    )(*outs)
     q_grad, k_grad, v_grad, weight_grad, row_loss, col_loss = outs
-    return q_grad[None], k_grad[None], v_grad[None], weight_grad, row_loss[0], col_loss[:, 0]
+    return q_grad[None], k_grad[None], v_grad[None], weight_grad, row_loss[0], col_loss[0]
 
 
 def solution(mesh):

time: 65.6 us -> 62.5 us (0.953)
  local copies, waits for them, and re-layouts: 5.56 us -> 0 us
  Pallas kernels: 57.9 us -> 61.1 us
    unnamed x15 -> x0, local copies, waits for them, and re-layouts: 5.56 us -> none
    pallas_call x0 -> x1, Pallas kernels: none -> 2.44 us  [shards(): pl.pallas_call(finish, out_shape=tuple((jax.ShapeDtypeStruct(x.shape, x.d...]
    pallas_call x1, Pallas kernels: 57.9 us -> 58.6 us  [shards(): pl.pallas_call(functools.partial(kernel, cfg), out_shape=(jax.ShapeDtypeS...]
where the time goes in v2:
time: 62.5 us; the launch traced here: 62.3 us
  Pallas kernels  61.1 us (98%)
  between operations  1.29 us (2%)
    pallas_call x1, Pallas kernels, shards(): pl.pallas_call(functools.partial(kernel, cfg), out_shape=(jax.ShapeDtypeS...  58.6 us
    pallas_call x1, Pallas kernels, shards(): pl.pallas_call(finish, out_shape=tuple((jax.ShapeDtypeStruct(x.shape, x.d...  2.44 us

profile of v2, /device:TPU:0, one launch (start us, length us, event | category | flops | bytes accessed | tf_op | source)
XLA Modules:
  0.0 62.3 jit_solution(12694790144050425740)
XLA Ops:
  1.3 58.6 %shard_map.136 = (bf16[512,512]{1,0:T(8,128)(2,1)}, bf16[512,128]{1,0:T(8,128)(2,1)}, bf16[512,128]{1,0:T(8,128)(2,1)}, bf16[128,2560]{1,0:T(8,128)(2,1)}, f32[1,128]{1,0:T(1,128)}, /*index=5*/f32[1,4]{1,0:T(1,128)}) custom-call(bf16[512,512]{1,0:T(8,128)(2,1)} %bitcast.11, bf16[512,128]{1,0:T(8,128)(2,1)} %bitcast.12, bf16[512,128]{1,0:T(8,128)(2,1)} %bitcast.13, ...), custom_call_target="tpu_custom_call" | custom-call | tf_op jit(solution)/shard_map/pallas_call | solution.py:521
  59.9 2.4 %shard_map.137 = (bf16[512,512]{1,0:T(8,128)(2,1)}, bf16[512,128]{1,0:T(8,128)(2,1)}, bf16[512,128]{1,0:T(8,128)(2,1)}, bf16[128,2560]{1,0:T(8,128)(2,1)}, f32[1,128]{1,0:T(1,128)}, /*index=5*/f32[1,4]{1,0:T(1,128)}) custom-call(bf16[512,512]{1,0:T(8,128)(2,1)} %get-tuple-element.18.refs_0_, bf16[512,128]{1,0:T(8,128)(2,1)} %get-tuple-element.19.refs_1_, ...), custom_call_target="tpu_custom_call" | custom-call | tf_op jit(solution)/shard_map/pallas_call | solution.py:576
